TPU v7x, 512 devices: a whole 4x4x16 slice. The times are simulated.
512 devices in a mesh: samp: 64 (over z, x), var: 8 (over y, core).
Axes of the slice: x: 4, y: 4, z: 16, core: 2. Of those that a mesh axis runs over, the one named last changes fastest.
Arguments:
- genotypes: bfloat16 [32768, 32768], P('samp', 'var'), may hold values from 0 to 2
- frequency: float32 [32768], P('var'), may hold values from 0.05 to 0.5
- start_block: float32 [32768, 16], P('var'), may hold values from -6 to 6
Outputs:
- loadings: float32 [32768, 16], P('var')
- scores: float32 [32768, 16], P('samp')
All inputs are finite; a program needn't handle non-finite values.
Results may differ from a plain program's by a relative error of at most 0.013.
Values may be sent and summed in bfloat16 or wider, within the bound.
A program may use at most 64 MiB of HBM per device.

v0:
```python
import jax
import jax.numpy as jnp
from jax import lax
from jax.sharding import PartitionSpec as P

VARIANTS = 32768
ITERS = 2


def project_rounded(standardized, narrow):
    partial_rows = jnp.dot(standardized, narrow, preferred_element_type=jnp.float32)
    return lax.psum(partial_rows.astype(jnp.bfloat16), "var")


def new_basis(variant_block, gram_matrix):
    factor = jnp.linalg.cholesky(gram_matrix)
    return jax.scipy.linalg.solve_triangular(factor, variant_block.T, lower=True).T


def local(genotypes, frequency, start_block):
    centre = 2.0 * frequency
    standardized = (
        (genotypes.astype(jnp.float32) - centre) / jnp.sqrt(centre * (1.0 - frequency))
    ).astype(jnp.bfloat16)
    narrow = start_block.astype(jnp.bfloat16)
    basis_cols = start_block
    for iteration in range(ITERS):
        sample_block = project_rounded(standardized, narrow)
        partial_terms = lax.dot_general(
            standardized, sample_block, (((0,), (0,)), ((), ())), preferred_element_type=jnp.float32
        )
        variant_block = lax.psum(partial_terms, "samp")
        local_gram = jnp.dot(variant_block.T, variant_block, precision=lax.Precision.HIGHEST)
        gram_matrix = lax.psum(local_gram, "var")
        basis_cols = new_basis(variant_block, gram_matrix)
        narrow = basis_cols.astype(jnp.bfloat16)
    scaling = jnp.sqrt(jnp.float32(VARIANTS))
    loadings = basis_cols * scaling
    partial_scores = jnp.dot(standardized, narrow, preferred_element_type=jnp.float32)
    scores = lax.psum(partial_scores, "var")
    return (loadings, scores)


def solution(mesh):
    placed = (P("samp", "var"), P("var"), P("var", None))
    return jax.shard_map(
        local,
        mesh=mesh,
        in_specs=placed,
        out_specs=(P("var", None), P("samp", None)),
        check_vma=False,
    )
```

profile of v0, /device:TPU:1, one launch (start us, length us, event | category | flops | bytes accessed | tf_op | source)
XLA Modules:
  0.0 668.9 jit_solution(5095902299904736016)
XLA Ops:
  7.2 0.0 all-reduce.3.cloned.1.call-start
  7.2 0.7 broadcast_multiply_fusion
  7.9 0.0 copy-start.1
  8.0 3.6 divide_convert_fusion
  11.5 0.0 copy-start
  11.5 1.9 copy-done
  13.4 0.0 copy-done.1
  13.4 1.2 convolution_convert_fusion.2
  14.7 28.4 %psum.49 = bf16[512,16]{1,0:T(8,128)(2,1)S(1)} all-reduce(bf16[512,16]{1,0:T(8,128)(2,1)S(1)} %convolution_convert_fusion.2), channel_id=1, replica_groups=mesh['samp'=64,'var'=8] {'var'}, use_global_device_ids=true, to_apply=%region_0.0 | all-reduce | flops 8192 | bytes 32768 | tf_op jit(solution)/shard_map/psum | solution.py:12
  43.1 3.6 fusion.14
  46.7 0.0 all-reduce.3.cloned.1.call-update
  46.7 0.0 all-reduce.5.cloned.1.call-start
  46.8 254.3 %all-reduce.3.cloned.1.call-done = f32[4096,16]{0,1:T(8,128)} async-done(((f32[4096,16]{0,1:T(8,128)}), f32[4096,16]{0,1:T(8,128)}) %all-reduce.3.cloned.1.call-update) | async-done | bytes 262160 | tf_op jit(solution)/shard_map/psum | solution.py:32
  301.1 1.5 fusion.15
  302.5 22.5 %psum.51 = f32[16,16]{0,1:T(8,128)S(1)} all-reduce(f32[16,16]{0,1:T(8,128)S(1)} %fusion.15), channel_id=1, replica_groups=mesh['samp'=64,'var'=8] {'var'}, use_global_device_ids=true, to_apply=%region_2.0 | all-reduce | flops 256 | bytes 2048 | tf_op jit(solution)/shard_map/psum | solution.py:34
  325.1 0.1 copy.6
  325.2 1.5 cholesky.44
  326.6 0.6 compare_reduce_fusion.1
  327.3 0.6 fusion.6
  327.9 1.2 custom-call.6
  329.2 1.4 convolution_convert_fusion
  330.5 3.4 convolution_convert_fusion.1
  334.0 22.2 %psum.52 = bf16[512,16]{1,0:T(8,128)(2,1)S(1)} all-reduce(bf16[512,16]{1,0:T(8,128)(2,1)S(1)} %convolution_convert_fusion.1), channel_id=1, replica_groups=mesh['samp'=64,'var'=8] {'var'}, use_global_device_ids=true, to_apply=%region_5.0 | all-reduce | flops 8192 | bytes 32768 | tf_op jit(solution)/shard_map/psum | solution.py:12
  356.2 3.6 fusion.16
  359.8 0.0 all-reduce.5.cloned.1.call-update
  359.8 247.3 %all-reduce.5.cloned.1.call-done = f32[4096,16]{0,1:T(8,128)} async-done(((f32[4096,16]{0,1:T(8,128)}), f32[4096,16]{0,1:T(8,128)}) %all-reduce.5.cloned.1.call-update) | async-done | bytes 262160 | tf_op jit(solution)/shard_map/psum | solution.py:32
  607.1 1.5 fusion.17
  608.6 22.5 %psum.54 = f32[16,16]{0,1:T(8,128)S(1)} all-reduce(f32[16,16]{0,1:T(8,128)S(1)} %fusion.17), channel_id=1, replica_groups=mesh['samp'=64,'var'=8] {'var'}, use_global_device_ids=true, to_apply=%region_7.10 | all-reduce | flops 256 | bytes 2048 | tf_op jit(solution)/shard_map/psum | solution.py:34
  631.1 0.1 copy.8
  631.2 1.5 cholesky.55
  632.7 0.6 compare_reduce_fusion
  633.3 0.6 fusion.7
  634.0 1.2 custom-call.7
  635.2 1.4 fusion
  636.6 3.4 fusion.3
  640.0 0.7 multiply_bitcast_fusion
  640.7 21.3 %psum.55 = f32[512,16]{0,1:T(8,128)} all-reduce(f32[512,16]{0,1:T(8,128)S(1)} %fusion.3), channel_id=1, replica_groups=mesh['samp'=64,'var'=8] {'var'}, use_global_device_ids=true, to_apply=%region_8.11 | all-reduce | flops 8192 | bytes 65536 | tf_op jit(solution)/shard_map/psum | solution.py:40
  (4 shorter events, 0.1 us)
Async XLA Ops:
  7.2 293.9 %all-reduce.3.cloned.1.call-start = ((), (), s32[]{:S(2)}) async-start(), calls=%async_computation | async-start | bytes 524288 | tf_op jit(solution)/shard_map/psum | solution.py:32
  7.9 5.5 copy-start.1
  11.5 1.9 copy-start
  46.7 560.4 %all-reduce.5.cloned.1.call-start = ((), (), s32[]{:S(2)}) async-start(), calls=%async_computation.1 | async-start | bytes 524288 | tf_op jit(solution)/shard_map/psum | solution.py:32
Sparse Core Ops, SparseCore 0:
  46.8 254.1 all-reduce.2
  359.9 247.1 all-reduce.4
where the time goes:
time: 670 us; the launch traced here: 669 us
  waiting for transfers between devices  502 us (75%)
  blocking collectives  117 us (17%)
  matrix products  20.9 us (3%)
  between operations  14.1 us (2%)
  other arithmetic  13 us (2%)
    psum x2, waiting for transfers between devices, local(): variant_block = lax.psum(partial_terms, 'samp')  502 us
    psum x2, blocking collectives, project_rounded(): return lax.psum(partial_rows.astype(jnp.bfloat16), 'var')  50.6 us
    psum x2, blocking collectives, local(): gram_matrix = lax.psum(local_gram, 'var')  45.1 us
    psum x1, blocking collectives, local(): scores = lax.psum(partial_scores, 'var')  21.3 us
  transfers between devices with their start and end apart: 2, of which 2 were waited for; matrix products, arithmetic and copies ran while one was open for 0% of the time, Pallas kernels for 0%

commit v1 on v0

v1 whole, which is shorter than its diff:
```python
import functools

import jax
import jax.numpy as jnp
from jax import lax
from jax.experimental import pallas as pl
from jax.experimental.pallas import tpu as pltpu
from jax.sharding import PartitionSpec as P

MESH = pl.DeviceIdType.MESH
F32, BF16 = jnp.float32, jnp.bfloat16
BLOCK = 16
VARIANTS = 32768
ROWS, COLS = 512, 4096
N_VAR = 8
NEAR, FAR = 16, 4
PIECE = COLS // NEAR
LOADS = 4
FIRST_WIRE, SECOND_WIRE = F32, F32


def split(a, terms):
    parts, rest = [], a
    for _ in range(terms):
        part = rest.astype(BF16)
        parts.append(part)
        rest = rest - part.astype(F32)
    return parts


def nt(a, b, **kw):
    return lax.dot_general(a, b, (((1,), (1,)), ((), ())), preferred_element_type=F32, **kw)


def row_of(a, k):
    return jnp.broadcast_to(a[k : k + 1, :], a.shape)


def inverse_factor(gram):
    shape = (BLOCK, 128)
    row = lax.broadcasted_iota(jnp.int32, shape, 0)
    lane = lax.broadcasted_iota(jnp.int32, shape, 1)
    columns = [jnp.broadcast_to(gram[:, j : j + 1], shape) for j in range(BLOCK)]
    inverse = jnp.where(row == lane, 1.0, 0.0).astype(F32)
    roots = jnp.zeros(shape, F32)
    for k in range(BLOCK):
        column = columns[k]
        pivot = row_of(column, k)
        factor = jnp.where(row > k, column / pivot, 0.0)
        roots = jnp.where(row == k, 1.0 / jnp.sqrt(pivot), roots)
        for j in range(k + 1, BLOCK):
            columns[j] = columns[j] - factor * row_of(column, j)
        inverse = inverse - factor * row_of(inverse, k)
    return inverse * roots


def kernel(
    g_hbm, freq_ref, start_ref, load_ref, score_ref,
    g, terms, gram_terms, centre, scale,
    p_first, p_slots, gram_slots,
    part_1, near_1, far_1, whole_1,
    part_2, near_2, far_2, whole_2,
    load_sems, pair_send, pair_recv, gram_send, gram_recv,
    near_send, near_recv, far_send, far_recv, whole_send, whole_recv,
):
    samp, var = lax.axis_index("samp"), lax.axis_index("var")
    z, x = lax.div(samp, 4), lax.rem(samp, 4)
    z_far, z_near = lax.div(z, 4), lax.rem(z, 4)
    y, core = lax.div(var, 2), lax.rem(var, 2)
    my_near = z_near * 4 + x

    var_peers = []
    for dy in (2, 1, 3, 0):
        for dc in (0, 1):
            if dy or dc:
                other = lax.rem(y + dy, 4) * 2 + lax.rem(core + dc, 2)
                var_peers.append((other, (samp, other)))
    near_peers = []
    for dz in (2, 1, 3, 0):
        for dx in (2, 1, 3, 0):
            if dz or dx:
                slot = lax.rem(z_near + dz, 4) * 4 + lax.rem(x + dx, 4)
                near_peers.append((slot, (z_far * 16 + slot, var)))
    far_peers = []
    for d in (2, 1, 3):
        slot = lax.rem(z_far + d, 4)
        far_peers.append((slot, (slot * 16 + my_near, var)))

    loads = []
    step = ROWS // LOADS
    for i in range(LOADS):
        rows = pl.ds(i * step, step)
        loads.append(pltpu.make_async_copy(g_hbm.at[rows, :], g.at[rows, :], load_sems.at[i]))
        loads[-1].start()

    barrier = pltpu.get_barrier_semaphore()
    everyone = far_peers + near_peers + var_peers
    for _, device in everyone:
        pl.semaphore_signal(barrier, 1, device_id=device, device_id_type=MESH)

    def copies(peers, source, target, mine, send, recv):
        return [
            (
                slot,
                pltpu.make_async_remote_copy(
                    src_ref=source(slot), dst_ref=target.at[mine], send_sem=send.at[slot], recv_sem=recv.at[mine],
                    device_id=device, device_id_type=MESH,
                ),
                pltpu.make_async_remote_copy(
                    src_ref=source(slot), dst_ref=target.at[slot], send_sem=send.at[slot], recv_sem=recv.at[slot],
                    device_id=device, device_id_type=MESH,
                ),
            )
            for slot, device in peers
        ]

    sent = []

    def start(group):
        for _, out, _ in group:
            out.start()
        sent.extend(group)

    def wait(group):
        for _, _, back in group:
            back.wait_recv()

    centre[...] = 2.0 * freq_ref[...]
    scale[...] = 1.0 / jnp.sqrt(centre[...] * (1.0 - centre[...] * 0.5))

    def fill(block, columns):
        scaled = block * scale[:, columns]
        high, low = split(scaled, 2)
        terms[0:BLOCK, columns] = high
        terms[BLOCK : 2 * BLOCK, columns] = low
        return jnp.sum((high.astype(F32) + low.astype(F32)) * centre[:, columns], axis=1, keepdims=True)

    def sample_product(rows, shift):
        both = nt(terms[...], g[rows, :])
        return both[0:BLOCK] + both[BLOCK:] - shift

    def exchange_samples(index, slots):
        group = copies(var_peers, lambda slot: slots.at[var], slots, var, pair_send.at[index], pair_recv.at[index])
        start(group)
        return group

    def total_of(slots, n):
        total = slots[0].astype(F32)
        for i in range(1, n):
            total = total + slots[i].astype(F32)
        return total

    def exchange_gram(index, whole):
        for b in range(NEAR):
            parts = split(whole[b].astype(F32), 3)
            for t in range(3):
                gram_terms[t * BLOCK : (t + 1) * BLOCK, b * PIECE : (b + 1) * PIECE] = parts[t]
        products = nt(gram_terms[...], gram_terms[...])
        gram = jnp.zeros((BLOCK, BLOCK), F32)
        for a, b in ((2, 2), (2, 1), (1, 2), (2, 0), (0, 2), (1, 1), (1, 0), (0, 1), (0, 0)):
            gram = gram + products[a * BLOCK : (a + 1) * BLOCK, b * BLOCK : (b + 1) * BLOCK]
        slots = gram_slots.at[index]
        slots[var, :, 0:BLOCK] = gram
        slots[var, :, BLOCK:] = jnp.zeros((BLOCK, 128 - BLOCK), F32)
        group = copies(var_peers, lambda slot: slots.at[var], slots, var, gram_send.at[index], gram_recv.at[index])
        start(group)
        return group

    def variant_pass(index, sample_block, part, near, far, whole):
        narrow = sample_block.astype(BF16)
        shift = jnp.sum(narrow.astype(F32), axis=1, keepdims=True)
        for b in range(NEAR):
            columns = slice(b * PIECE, (b + 1) * PIECE)
            product = jnp.dot(narrow, g[:, columns], preferred_element_type=F32)
            part[b] = ((product - shift * centre[:, columns]) * scale[:, columns]).astype(part.dtype)
        group = copies(near_peers, lambda slot: part.at[slot], near, my_near, near_send.at[index], near_recv.at[index])
        start(group)
        total = part[my_near].astype(F32)
        for slot, _, back in reversed(group):
            back.wait_recv()
            total = total + near[slot].astype(F32)
        far[z_far] = total.astype(far.dtype)
        group = copies(far_peers, lambda slot: far.at[z_far], far, z_far, far_send.at[index], far_recv.at[index])
        start(group)
        wait(group)
        whole[my_near] = total_of(far, FAR).astype(whole.dtype)
        group = copies(near_peers, lambda slot: whole.at[my_near], whole, my_near, whole_send.at[index], whole_recv.at[index])
        start(group)
        wait(group)

    def sample_pass(index, whole):
        shift = jnp.zeros((BLOCK, 1), F32)
        for b in range(NEAR):
            shift = shift + fill(whole[b].astype(F32), slice(b * PIECE, (b + 1) * PIECE))
        slots = p_slots.at[index]
        slots[var] = sample_product(slice(None), shift)
        return exchange_samples(index + 1, slots)

    def whitener(index, group):
        wait(group)
        return inverse_factor(total_of(gram_slots.at[index], N_VAR)[:, 0:BLOCK])[:, 0:BLOCK]

    shift = fill(start_ref[...].astype(BF16).astype(F32), slice(None))
    for i in range(LOADS):
        loads[i].wait()
        rows = slice(i * step, (i + 1) * step)
        p_first[var, :, rows] = sample_product(rows, shift).astype(BF16)
    pl.semaphore_wait(barrier, len(everyone))
    group = exchange_samples(0, p_first)
    wait(group)
    variant_pass(0, total_of(p_first, N_VAR), part_1, near_1, far_1, whole_1)

    gram_group = exchange_gram(0, whole_1)
    group = sample_pass(0, whole_1)
    whiten = whitener(0, gram_group)
    wait(group)
    sample_block = jnp.dot(whiten, total_of(p_slots.at[0], N_VAR), precision=lax.Precision.HIGHEST, preferred_element_type=F32)
    variant_pass(1, sample_block, part_2, near_2, far_2, whole_2)

    gram_group = exchange_gram(1, whole_2)
    group = sample_pass(1, whole_2)
    whiten = whitener(1, gram_group)
    scaled = whiten * jnp.sqrt(jnp.float32(VARIANTS))
    for b in range(NEAR):
        load_ref[:, b * PIECE : (b + 1) * PIECE] = jnp.dot(
            scaled, whole_2[b].astype(F32), precision=lax.Precision.HIGHEST, preferred_element_type=F32
        )
    wait(group)
    score_ref[...] = jnp.dot(whiten, total_of(p_slots.at[1], N_VAR), precision=lax.Precision.HIGHEST, preferred_element_type=F32)
    for _, out, _ in sent:
        out.wait_send()


def local(genotypes, frequency, start_block):
    piece = (BLOCK, PIECE)
    scratch = [
        pltpu.VMEM((ROWS, COLS), BF16),
        pltpu.VMEM((2 * BLOCK, COLS), BF16),
        pltpu.VMEM((3 * BLOCK, COLS), BF16),
        pltpu.VMEM((1, COLS), F32),
        pltpu.VMEM((1, COLS), F32),
        pltpu.VMEM((N_VAR, BLOCK, ROWS), BF16),
        pltpu.VMEM((2, N_VAR, BLOCK, ROWS), F32),
        pltpu.VMEM((2, N_VAR, BLOCK, 128), F32),
    ]
    for wire in (FIRST_WIRE, SECOND_WIRE):
        scratch += [pltpu.VMEM((n,) + piece, wire) for n in (NEAR, NEAR, FAR, NEAR)]
    scratch += [pltpu.SemaphoreType.DMA((LOADS,))]
    for n in ((3, N_VAR), (2, N_VAR), (2, NEAR), (2, FAR), (2, NEAR)):
        scratch += [pltpu.SemaphoreType.DMA(n)] * 2
    vmem = pl.BlockSpec(memory_space=pltpu.VMEM)
    loadings, scores = pl.pallas_call(
        kernel,
        name="subspace",
        out_shape=(jax.ShapeDtypeStruct((BLOCK, COLS), F32), jax.ShapeDtypeStruct((BLOCK, ROWS), F32)),
        in_specs=[pl.BlockSpec(memory_space=pltpu.HBM), vmem, vmem],
        out_specs=(vmem, vmem),
        scratch_shapes=scratch,
        compiler_params=pltpu.CompilerParams(collective_id=0, has_side_effects=True, vmem_limit_bytes=48 << 20),
        cost_estimate=pl.CostEstimate(flops=5 * 2 * ROWS * COLS * BLOCK, bytes_accessed=2 * ROWS * COLS, transcendentals=0),
    )(genotypes, frequency.reshape(1, COLS), start_block.T)
    return loadings.T, scores.T


def solution(mesh):
    return jax.shard_map(
        local,
        mesh=mesh,
        in_specs=(P("samp", "var"), P("var"), P("var", None)),
        out_specs=(P("var", None), P("samp", None)),
        check_vma=False,
    )
```

time: 670 us -> 87.7 us (0.13)
  waiting for transfers between devices: 502 us -> 0 us
  blocking collectives: 117 us -> 0 us
  Pallas kernels: 0 us -> 81.6 us
  matrix products: 20.9 us -> 0 us
  between operations: 14.1 us -> 0.65 us
  other arithmetic: 13 us -> 0 us
    psum x2 -> x0, waiting for transfers between devices: 502 us -> none  [local(): variant_block = lax.psum(partial_terms, 'samp')]
    psum x5 -> x0, blocking collectives: 117 us -> none  [the longest x2 50.6 us: project_rounded(): return lax.psum(partial_rows.astype(jnp.bfloat16), 'var')]
    pallas_call x0 -> x1, Pallas kernels: none -> 81.6 us  [local(): pl.pallas_call(kernel, name='subspace', out_shape=(jax.ShapeDtypeStruct((...]
    dot_general x7 -> x0, matrix products: 18.1 us -> none  [the longest x2 7.18 us: local(): lax.dot_general(standardized, sample_block, (((0,), (0,)), ((), ())), pre...]
    another operation x10 -> x0, other arithmetic: 8.01 us -> none  [the longest x6 4.26 us: new_basis(): factor = jnp.linalg.cholesky(gram_matrix)]
  transfers between devices with their start and end apart: 2 -> 0, of which waited for: 2 -> 0; matrix products, arithmetic and copies ran while one was open for 0% -> 0% of each run, Pallas kernels for 0% -> 0%
where the time goes in v1:
time: 87.7 us; the launch traced here: 87.4 us
  Pallas kernels  81.6 us (93%)
  local copies, waits for them, and re-layouts  5.17 us (6%)
    pallas_call x1, Pallas kernels, local(): pl.pallas_call(kernel, name='subspace', out_shape=(jax.ShapeDtypeStruct((...  81.6 us
    unnamed x8, local copies, waits for them, and re-layouts  5.17 us

profile of v1, /device:TPU:1, one launch (start us, length us, event | category | flops | bytes accessed | tf_op | source)
XLA Modules:
  0.0 87.4 jit_solution(9999796111010062021)
XLA Ops:
  0.6 0.0 copy-start
  0.6 2.2 %copy-done = bf16[512,4096]{1,0:T(8,128)(2,1)S(1)} copy-done((bf16[512,4096]{1,0:T(8,128)(2,1)S(1)}, bf16[512,4096]{1,0:T(8,128)(2,1)}, u32[]{:S(2)}) %copy-start) | copy-done | bytes 4194328
  2.8 0.0 copy-start.1
  2.8 0.9 %copy-done.1 = f32[4096,16]{0,1:T(8,128)S(1)} copy-done((f32[4096,16]{0,1:T(8,128)S(1)}, f32[4096,16]{0,1:T(8,128)}, u32[]{:S(2)}) %copy-start.1) | copy-done | bytes 262168
  3.8 0.0 copy-start.2
  3.8 0.7 copy-done.2
  4.5 81.6 %subspace.1 = (f32[16,4096]{1,0:T(8,128)S(1)}, f32[16,512]{1,0:T(8,128)S(1)}) custom-call(bf16[512,4096]{1,0:T(8,128)(2,1)S(1)} %copy-done, f32[1,4096]{1,0:T(1,128)S(1)} %bitcast.7, f32[16,4096]{1,0:T(8,128)S(1)} %bitcast.4), custom_call_target="tpu_custom_call" | custom-call | flops 335544320 | bytes 4194304 | tf_op jit(solution)/shard_map/subspace/pallas_call | solution.py:252
  86.1 0.7 copy.7
  86.8 0.6 copy.8
Async XLA Ops:
  0.6 2.2 %copy-start = (bf16[512,4096]{1,0:T(8,128)(2,1)S(1)}, bf16[512,4096]{1,0:T(8,128)(2,1)}, u32[]{:S(2)}) copy-start(bf16[512,4096]{1,0:T(8,128)(2,1)} %g_hbm.1) | copy-start | bytes 12582916
  2.8 0.9 %copy-start.1 = (f32[4096,16]{0,1:T(8,128)S(1)}, f32[4096,16]{0,1:T(8,128)}, u32[]{:S(2)}) copy-start(f32[4096,16]{0,1:T(8,128)} %param.5) | copy-start | bytes 786436
  3.8 0.7 copy-start.2

commit v2 on v1

v2 whole, which is shorter than its diff:
```python
import jax
import jax.numpy as jnp
from jax import lax
from jax.experimental import pallas as pl
from jax.experimental.pallas import tpu as pltpu
from jax.sharding import PartitionSpec as P

MESH = pl.DeviceIdType.MESH
F32, BF16 = jnp.float32, jnp.bfloat16
BLOCK = 16
VARIANTS = 32768
ROWS, COLS = 512, 4096
N_VAR = 8
NEAR, FAR = 16, 4
PIECE = COLS // NEAR
LOADS = 8
FIRST_WIRE, SECOND_WIRE = F32, BF16


def split(a, terms):
    parts, rest = [], a
    for _ in range(terms):
        part = rest.astype(BF16)
        parts.append(part)
        rest = rest - part.astype(F32)
    return parts


def nt(a, b):
    return lax.dot_general(a, b, (((1,), (1,)), ((), ())), preferred_element_type=F32)


def full(a, b):
    return jnp.dot(a, b, precision=lax.Precision.HIGHEST, preferred_element_type=F32)


def row_of(a, k):
    return jnp.broadcast_to(a[k : k + 1, :], a.shape)


def inverse_factor(gram):
    shape = (BLOCK, 128)
    row = lax.broadcasted_iota(jnp.int32, shape, 0)
    lane = lax.broadcasted_iota(jnp.int32, shape, 1)
    columns = [jnp.broadcast_to(gram[:, j : j + 1], shape) for j in range(BLOCK)]
    inverse = jnp.where(row == lane, 1.0, 0.0).astype(F32)
    roots = jnp.zeros(shape, F32)
    for k in range(BLOCK):
        column = columns[k]
        pivot = row_of(column, k)
        factor = jnp.where(row > k, column / pivot, 0.0)
        roots = jnp.where(row == k, 1.0 / jnp.sqrt(pivot), roots)
        for j in range(k + 1, BLOCK):
            columns[j] = columns[j] - factor * row_of(column, j)
        inverse = inverse - factor * row_of(inverse, k)
    return inverse * roots


def kernel(
    g_hbm, freq_hbm, start_hbm, load_ref, score_ref,
    g, g_t, start_block, frequency, centre, scale,
    p_first, p_slots, gram_rows, gram_slots,
    part_1, near_1, far_1, whole_1,
    part_2, near_2, far_2, whole_2,
    load_sems, pair_send, pair_recv, gram_send, gram_recv,
    near_send, near_recv, far_send, far_recv, whole_send, whole_recv, opposite_sem, diagonal_sem,
):
    samp, var = lax.axis_index("samp"), lax.axis_index("var")
    z, x = lax.div(samp, 4), lax.rem(samp, 4)
    z_far, z_near = lax.div(z, 4), lax.rem(z, 4)
    y, core = lax.div(var, 2), lax.rem(var, 2)
    my_near = z_near * 4 + x

    var_peers = []
    for dy in (2, 1, 3, 0):
        for dc in (0, 1):
            if dy or dc:
                other = lax.rem(y + dy, 4) * 2 + lax.rem(core + dc, 2)
                var_peers.append((other, (samp, other)))
    near_peers = []
    for dz in (2, 1, 3, 0):
        for dx in (2, 1, 3, 0):
            if dz or dx:
                slot = lax.rem(z_near + dz, 4) * 4 + lax.rem(x + dx, 4)
                near_peers.append((slot, (z_far * 16 + slot, var)))
    far_peers = []
    for d in (2, 1, 3):
        slot = lax.rem(z_far + d, 4)
        far_peers.append((slot, (slot * 16 + my_near, var)))

    barrier = pltpu.get_barrier_semaphore()
    along_x = [near_peers[i] for i in (12, 13, 14)]
    along_z = [near_peers[i] for i in (3, 7, 11)]
    everyone = far_peers[1:] + along_z + along_x + var_peers
    for _, device in everyone:
        pl.semaphore_signal(barrier, 1, device_id=device, device_id_type=MESH)

    loads = [
        pltpu.make_async_copy(freq_hbm, frequency, load_sems.at[0]),
        pltpu.make_async_copy(start_hbm, start_block, load_sems.at[1]),
    ]
    step = COLS // LOADS
    for i in range(LOADS):
        columns = pl.ds(i * step, step)
        loads.append(pltpu.make_async_copy(g_hbm.at[:, columns], g.at[:, columns], load_sems.at[i + 2]))
    for load in loads:
        load.start()

    def copies(peers, source, target, mine, send, recv):
        return [
            (
                slot,
                pltpu.make_async_remote_copy(
                    src_ref=source(slot), dst_ref=target.at[mine], send_sem=send.at[slot], recv_sem=recv.at[mine],
                    device_id=device, device_id_type=MESH,
                ),
                pltpu.make_async_remote_copy(
                    src_ref=source(slot), dst_ref=target.at[slot], send_sem=send.at[slot], recv_sem=recv.at[slot],
                    device_id=device, device_id_type=MESH,
                ),
            )
            for slot, device in peers
        ]

    sent = []

    def start(group):
        for _, out, _ in group:
            out.start()
        sent.extend(group)

    def wait(group):
        for _, _, back in group:
            back.wait_recv()

    def scaled_terms(block, b):
        high, low = split(block * scale[b], 2)
        return jnp.concatenate([high, low], axis=0), (high.astype(F32) + low.astype(F32)) * centre[b]

    def sample_product(total, shift):
        return total[0:BLOCK] + total[BLOCK:] - jnp.sum(shift, axis=1, keepdims=True)

    def exchange_samples(index, slots):
        group = copies(var_peers, lambda slot: slots.at[var], slots, var, pair_send.at[index], pair_recv.at[index])
        start(group)
        return group

    def total_of(slots, n):
        total = slots[0].astype(F32)
        for i in range(1, n):
            total = total + slots[i].astype(F32)
        return total

    def variant_pass(index, sample_block, part, near, far, whole):
        narrow = sample_block.astype(BF16)
        shift = jnp.sum(narrow.astype(F32), axis=1, keepdims=True)
        for b in range(NEAR):
            product = jnp.dot(narrow, g[:, b * PIECE : (b + 1) * PIECE], preferred_element_type=F32)
            part[b] = ((product - shift * centre[b]) * scale[b]).astype(part.dtype)
        if index == 0:
            pl.semaphore_wait(diagonal_sem, len(along_x))
        group = copies(near_peers, lambda slot: part.at[slot], near, my_near, near_send.at[index], near_recv.at[index])
        start(group)
        total = part[my_near].astype(F32)
        for slot, _, back in reversed(group):
            back.wait_recv()
            total = total + near[slot].astype(F32)
        far[z_far] = total.astype(far.dtype)
        if index == 0:
            pl.semaphore_wait(opposite_sem, 1)
        group = copies(far_peers, lambda slot: far.at[z_far], far, z_far, far_send.at[index], far_recv.at[index])
        start(group)
        wait(group)
        whole[my_near] = total_of(far, FAR).astype(whole.dtype)
        group = copies(near_peers, lambda slot: whole.at[my_near], whole, my_near, whole_send.at[index], whole_recv.at[index])
        start(group)
        return group

    def sample_pass(index, whole, arriving):
        exact = whole.dtype == BF16
        total, shift = jnp.zeros((2 * BLOCK, ROWS), F32), jnp.zeros((BLOCK, PIECE), F32)
        for dz in (0, 1, 3, 2):
            z_row = lax.rem(z_near + dz, 4)
            first = 4 * (2, 1, 3, 0).index(dz)
            wait(arriving[first : first + 4])
            blocks = [whole[z_row * 4 + i].astype(F32) for i in range(4)]
            gram = jnp.zeros((BLOCK, BLOCK), F32)
            for block in blocks:
                if exact:
                    terms = block.astype(BF16)
                    gram = gram + nt(terms, terms)
                else:
                    high, middle, low = split(block, 3)
                    gram = gram + nt(
                        jnp.concatenate([high, high, middle, high, low, middle], axis=1),
                        jnp.concatenate([high, middle, high, low, high, middle], axis=1),
                    )
            gram_rows[z_row, :, 0:BLOCK] = gram
            rows = []
            for i, block in enumerate(blocks):
                terms, shifted = scaled_terms(block, z_row * 4 + i)
                rows.append(terms)
                shift = shift + shifted
            depth = 4 * PIECE
            total = total + jnp.dot(
                jnp.concatenate(rows, axis=1),
                g_t[pl.ds(pl.multiple_of(z_row * depth, depth), depth), :],
                preferred_element_type=F32,
            )
        gram = gram_rows[0, :, 0:BLOCK]
        for i in range(1, 4):
            gram = gram + gram_rows[i, :, 0:BLOCK]
        whole_gram = gram_slots.at[index]
        whole_gram[var, :, 0:BLOCK] = gram
        whole_gram[var, :, BLOCK:] = jnp.zeros((BLOCK, 128 - BLOCK), F32)
        gram_group = copies(
            var_peers, lambda slot: whole_gram.at[var], whole_gram, var, gram_send.at[index], gram_recv.at[index]
        )
        start(gram_group)
        slots = p_slots.at[index]
        slots[var] = sample_product(total, shift)
        group = exchange_samples(index + 1, slots)
        wait(gram_group)
        return group, inverse_factor(total_of(whole_gram, N_VAR)[:, 0:BLOCK])[:, 0:BLOCK]

    loads[0].wait()
    centre[...] = 2.0 * frequency[...]
    scale[...] = 1.0 / jnp.sqrt(centre[...] * (1.0 - frequency[...]))
    loads[1].wait()
    total, shift = jnp.zeros((2 * BLOCK, ROWS), F32), jnp.zeros((BLOCK, PIECE), F32)
    for i in range(LOADS):
        loads[i + 2].wait()
        for b in range(i * NEAR // LOADS, (i + 1) * NEAR // LOADS):
            columns = slice(b * PIECE, (b + 1) * PIECE)
            terms, shifted = scaled_terms(start_block[:, columns].astype(BF16).astype(F32), b)
            total = total + nt(terms, g[:, columns])
            shift = shift + shifted
    p_first[var] = sample_product(total, shift).astype(BF16)
    pl.semaphore_wait(barrier, len(everyone))
    pl.semaphore_signal(opposite_sem, 1, device_id=far_peers[1][1], device_id_type=MESH)
    for _, device in along_x:
        pl.semaphore_signal(diagonal_sem, 1, device_id=device, device_id_type=MESH)
    group = exchange_samples(0, p_first)
    for b in range(NEAR):
        g_t[b * PIECE : (b + 1) * PIECE, :] = g[:, b * PIECE : (b + 1) * PIECE].T
    wait(group)
    arriving = variant_pass(0, total_of(p_first, N_VAR), part_1, near_1, far_1, whole_1)

    group, whiten = sample_pass(0, whole_1, arriving)
    wait(group)
    sample_block = full(whiten, total_of(p_slots.at[0], N_VAR))
    arriving = variant_pass(1, sample_block, part_2, near_2, far_2, whole_2)

    group, whiten = sample_pass(1, whole_2, arriving)
    scaled = whiten * jnp.sqrt(jnp.float32(VARIANTS))
    for b in range(NEAR):
        load_ref[:, b * PIECE : (b + 1) * PIECE] = full(scaled, whole_2[b].astype(F32))
    wait(group)
    score_ref[...] = full(whiten, total_of(p_slots.at[1], N_VAR))
    for _, out, _ in sent:
        out.wait_send()


def local(genotypes, frequency, start_block):
    piece = (BLOCK, PIECE)
    row = (NEAR, 1, PIECE)
    scratch = [
        pltpu.VMEM((ROWS, COLS), BF16),
        pltpu.VMEM((COLS, ROWS), BF16),
        pltpu.VMEM((BLOCK, COLS), F32),
        pltpu.VMEM(row, F32),
        pltpu.VMEM(row, F32),
        pltpu.VMEM(row, F32),
        pltpu.VMEM((N_VAR, BLOCK, ROWS), BF16),
        pltpu.VMEM((2, N_VAR, BLOCK, ROWS), F32),
        pltpu.VMEM((4, BLOCK, 128), F32),
        pltpu.VMEM((2, N_VAR, BLOCK, 128), F32),
    ]
    for wire in (FIRST_WIRE, SECOND_WIRE):
        scratch += [pltpu.VMEM((n,) + piece, wire) for n in (NEAR, NEAR, FAR, NEAR)]
    scratch += [pltpu.SemaphoreType.DMA((LOADS + 2,))]
    for n in ((3, N_VAR), (2, N_VAR), (2, NEAR), (2, FAR), (2, NEAR)):
        scratch += [pltpu.SemaphoreType.DMA(n)] * 2
    scratch += [pltpu.SemaphoreType.REGULAR] * 2
    vmem, hbm = pl.BlockSpec(memory_space=pltpu.VMEM), pl.BlockSpec(memory_space=pl.ANY)
    loadings, scores = pl.pallas_call(
        kernel,
        name="subspace",
        out_shape=(pltpu.VMEM((BLOCK, COLS), F32), pltpu.VMEM((BLOCK, ROWS), F32)),
        in_specs=[hbm, hbm, hbm],
        out_specs=(vmem, vmem),
        scratch_shapes=scratch,
        compiler_params=pltpu.CompilerParams(collective_id=0, has_side_effects=True, vmem_limit_bytes=48 << 20),
        cost_estimate=pl.CostEstimate(flops=5 * 2 * ROWS * COLS * BLOCK, bytes_accessed=2 * ROWS * COLS, transcendentals=0),
    )(*(pltpu.with_memory_space_constraint(a, pltpu.HBM) for a in (genotypes, frequency.reshape(row), start_block.T)))
    return loadings.T, scores.T


def solution(mesh):
    return jax.shard_map(
        local,
        mesh=mesh,
        in_specs=(P("samp", "var"), P("var"), P("var", None)),
        out_specs=(P("var", None), P("samp", None)),
        check_vma=False,
    )
```

time: 87.7 us -> 74.6 us (0.85)
  Pallas kernels: 81.6 us -> 72.5 us
  local copies, waits for them, and re-layouts: 5.17 us -> 1.32 us
    pallas_call x1, Pallas kernels: 81.6 us -> 72.5 us  [local(): pl.pallas_call(kernel, name='subspace', out_shape=(pltpu.VMEM((BLOCK, COL...]
    unnamed x8 -> x2, local copies, waits for them, and re-layouts: 5.17 us -> 1.32 us
where the time goes in v2:
time: 74.6 us; the launch traced here: 74.4 us
  Pallas kernels  72.5 us (97%)
  local copies, waits for them, and re-layouts  1.32 us (2%)
    pallas_call x1, Pallas kernels, local(): pl.pallas_call(kernel, name='subspace', out_shape=(pltpu.VMEM((BLOCK, COL...  72.5 us

profile of v2, /device:TPU:1, one launch (start us, length us, event | category | flops | bytes accessed | tf_op | source)
XLA Modules:
  0.0 74.4 jit_solution(6438562857398247415)
XLA Ops:
  0.6 72.5 %subspace.1 = (f32[16,4096]{1,0:T(8,128)S(1)}, f32[16,512]{1,0:T(8,128)S(1)}) custom-call(bf16[512,4096]{1,0:T(8,128)(2,1)} %g_hbm.1, f32[16,1,256]{2,1,0:T(1,128)} %bitcast.7, f32[16,4096]{1,0:T(8,128)} %bitcast.6), custom_call_target="tpu_custom_call" | custom-call | flops 335544320 | bytes 4194304 | tf_op jit(solution)/shard_map/subspace/pallas_call | solution.py:286
  73.1 0.7 copy.7
  73.8 0.6 copy.8

commit v3 on v2

--- a/solution.py
+++ b/solution.py
@@ -12,9 +12,9 @@
 ROWS, COLS = 512, 4096
 N_VAR = 8
 NEAR, FAR = 16, 4
-PIECE = COLS // NEAR
+PARTS = 2
+PIECE = COLS // NEAR // PARTS
 LOADS = 8
-FIRST_WIRE, SECOND_WIRE = F32, BF16
 
 
 def split(a, terms):
@@ -60,8 +60,7 @@
     g_hbm, freq_hbm, start_hbm, load_ref, score_ref,
     g, g_t, start_block, frequency, centre, scale,
     p_first, p_slots, gram_rows, gram_slots,
-    part_1, near_1, far_1, whole_1,
-    part_2, near_2, far_2, whole_2,
+    part, near, far, whole,
     load_sems, pair_send, pair_recv, gram_send, gram_recv,
     near_send, near_recv, far_send, far_recv, whole_send, whole_recv, opposite_sem, diagonal_sem,
 ):
@@ -77,20 +76,21 @@
             if dy or dc:
                 other = lax.rem(y + dy, 4) * 2 + lax.rem(core + dc, 2)
                 var_peers.append((other, (samp, other)))
+    z_at = [z_near, z_near + 1 - 2 * lax.rem(z_near, 2), lax.rem(z_near + 2, 4), 3 - z_near]
+    steps = [(a, b) for a in range(4) for b in range(4) if a or b]
+    steps.sort(key=lambda step: -step[0] - (0, 1, 2, 1.6)[step[1]])
     near_peers = []
-    for dz in (2, 1, 3, 0):
-        for dx in (2, 1, 3, 0):
-            if dz or dx:
-                slot = lax.rem(z_near + dz, 4) * 4 + lax.rem(x + dx, 4)
-                near_peers.append((slot, (z_far * 16 + slot, var)))
+    for a, b in steps:
+        slot = z_at[a] * 4 + lax.rem(x + b, 4)
+        near_peers.append((slot, (z_far * 16 + slot, var)))
     far_peers = []
     for d in (2, 1, 3):
         slot = lax.rem(z_far + d, 4)
         far_peers.append((slot, (slot * 16 + my_near, var)))
 
     barrier = pltpu.get_barrier_semaphore()
-    along_x = [near_peers[i] for i in (12, 13, 14)]
-    along_z = [near_peers[i] for i in (3, 7, 11)]
+    along_x = [near_peers[i] for i, (a, b) in enumerate(steps) if a == 0]
+    along_z = [near_peers[i] for i, (a, b) in enumerate(steps) if b == 0]
     everyone = far_peers[1:] + along_z + along_x + var_peers
     for _, device in everyone:
         pl.semaphore_signal(barrier, 1, device_id=device, device_id_type=MESH)
@@ -151,67 +151,75 @@
             total = total + slots[i].astype(F32)
         return total
 
-    def variant_pass(index, sample_block, part, near, far, whole):
+    def variant_pass(index, sample_block):
         narrow = sample_block.astype(BF16)
         shift = jnp.sum(narrow.astype(F32), axis=1, keepdims=True)
-        for b in range(NEAR):
-            product = jnp.dot(narrow, g[:, b * PIECE : (b + 1) * PIECE], preferred_element_type=F32)
-            part[b] = ((product - shift * centre[b]) * scale[b]).astype(part.dtype)
-        if index == 0:
-            pl.semaphore_wait(diagonal_sem, len(along_x))
-        group = copies(near_peers, lambda slot: part.at[slot], near, my_near, near_send.at[index], near_recv.at[index])
-        start(group)
-        total = part[my_near].astype(F32)
-        for slot, _, back in reversed(group):
-            back.wait_recv()
-            total = total + near[slot].astype(F32)
-        far[z_far] = total.astype(far.dtype)
-        if index == 0:
-            pl.semaphore_wait(opposite_sem, 1)
-        group = copies(far_peers, lambda slot: far.at[z_far], far, z_far, far_send.at[index], far_recv.at[index])
-        start(group)
-        wait(group)
-        whole[my_near] = total_of(far, FAR).astype(whole.dtype)
-        group = copies(near_peers, lambda slot: whole.at[my_near], whole, my_near, whole_send.at[index], whole_recv.at[index])
-        start(group)
-        return group
-
-    def sample_pass(index, whole, arriving):
-        exact = whole.dtype == BF16
+        stages = [index * PARTS + h for h in range(PARTS)]
+        groups = []
+        for h, stage in enumerate(stages):
+            for b in range(0, NEAR, 2):
+                first = h * NEAR + b
+                product = jnp.dot(narrow, g[:, first * PIECE : (first + 2) * PIECE], preferred_element_type=F32)
+                for i in range(2):
+                    piece = product[:, i * PIECE : (i + 1) * PIECE]
+                    part[stage, b + i] = (piece - shift * centre[first + i]) * scale[first + i]
+            if stage == 0:
+                pl.semaphore_wait(diagonal_sem, len(along_x))
+            group = copies(
+                near_peers, lambda slot: part.at[stage, slot], near.at[stage], my_near, near_send.at[stage], near_recv.at[stage]
+            )
+            start(group)
+            groups.append(group)
+        far_groups = []
+        for stage, group in zip(stages, groups):
+            total = part[stage, my_near]
+            for slot, _, back in reversed(group):
+                back.wait_recv()
+                total = total + near[stage, slot]
+            far[stage, z_far] = total
+            if stage == 0:
+                pl.semaphore_wait(opposite_sem, 1)
+            group = copies(
+                far_peers, lambda slot: far.at[stage, z_far], far.at[stage], z_far, far_send.at[stage], far_recv.at[stage]
+            )
+            start(group)
+            far_groups.append(group)
+        groups = []
+        for stage, group in zip(stages, far_groups):
+            wait(group)
+            whole[stage, my_near] = total_of(far.at[stage], FAR)
+            group = copies(
+                near_peers, lambda slot: whole.at[stage, my_near], whole.at[stage], my_near,
+                whole_send.at[stage], whole_recv.at[stage],
+            )
+            start(group)
+            groups.append(group)
+        return groups
+
+    def sample_pass(index, arriving):
         total, shift = jnp.zeros((2 * BLOCK, ROWS), F32), jnp.zeros((BLOCK, PIECE), F32)
-        for dz in (0, 1, 3, 2):
-            z_row = lax.rem(z_near + dz, 4)
-            first = 4 * (2, 1, 3, 0).index(dz)
-            wait(arriving[first : first + 4])
-            blocks = [whole[z_row * 4 + i].astype(F32) for i in range(4)]
-            gram = jnp.zeros((BLOCK, BLOCK), F32)
-            for block in blocks:
-                if exact:
-                    terms = block.astype(BF16)
-                    gram = gram + nt(terms, terms)
-                else:
-                    high, middle, low = split(block, 3)
-                    gram = gram + nt(
-                        jnp.concatenate([high, high, middle, high, low, middle], axis=1),
-                        jnp.concatenate([high, middle, high, low, high, middle], axis=1),
-                    )
-            gram_rows[z_row, :, 0:BLOCK] = gram
-            rows = []
-            for i, block in enumerate(blocks):
-                terms, shifted = scaled_terms(block, z_row * 4 + i)
-                rows.append(terms)
-                shift = shift + shifted
-            depth = 4 * PIECE
-            total = total + jnp.dot(
-                jnp.concatenate(rows, axis=1),
-                g_t[pl.ds(pl.multiple_of(z_row * depth, depth), depth), :],
-                preferred_element_type=F32,
-            )
-        gram = gram_rows[0, :, 0:BLOCK]
-        for i in range(1, 4):
-            gram = gram + gram_rows[i, :, 0:BLOCK]
+        depth = 4 * PIECE
+        for h in range(PARTS):
+            for a in range(4):
+                wait([arriving[h][i] for i, step in enumerate(steps) if step[0] == a])
+                blocks = [whole[index * PARTS + h, z_at[a] * 4 + i] for i in range(4)]
+                high, middle, low = split(jnp.concatenate(blocks, axis=1), 3)
+                gram_rows[h * 4 + z_at[a], :, 0:BLOCK] = nt(
+                    jnp.concatenate([high, high, middle, high, low, middle], axis=1),
+                    jnp.concatenate([high, middle, high, low, high, middle], axis=1),
+                )
+                rows = []
+                for i, block in enumerate(blocks):
+                    terms, shifted = scaled_terms(block, h * NEAR + z_at[a] * 4 + i)
+                    rows.append(terms)
+                    shift = shift + shifted
+                total = total + jnp.dot(
+                    jnp.concatenate(rows, axis=1),
+                    g_t[pl.ds(pl.multiple_of((h * 4 + z_at[a]) * depth, depth), depth), :],
+                    preferred_element_type=F32,
+                )
         whole_gram = gram_slots.at[index]
-        whole_gram[var, :, 0:BLOCK] = gram
+        whole_gram[var, :, 0:BLOCK] = sum((gram_rows[i, :, 0:BLOCK] for i in range(1, 4 * PARTS)), gram_rows[0, :, 0:BLOCK])
         whole_gram[var, :, BLOCK:] = jnp.zeros((BLOCK, 128 - BLOCK), F32)
         gram_group = copies(
             var_peers, lambda slot: whole_gram.at[var], whole_gram, var, gram_send.at[index], gram_recv.at[index]
@@ -230,31 +238,34 @@
     total, shift = jnp.zeros((2 * BLOCK, ROWS), F32), jnp.zeros((BLOCK, PIECE), F32)
     for i in range(LOADS):
         loads[i + 2].wait()
-        for b in range(i * NEAR // LOADS, (i + 1) * NEAR // LOADS):
+        rows = []
+        for b in range(i * step // PIECE, (i + 1) * step // PIECE):
             columns = slice(b * PIECE, (b + 1) * PIECE)
             terms, shifted = scaled_terms(start_block[:, columns].astype(BF16).astype(F32), b)
-            total = total + nt(terms, g[:, columns])
+            rows.append(terms)
             shift = shift + shifted
+        total = total + nt(jnp.concatenate(rows, axis=1), g[:, i * step : (i + 1) * step])
     p_first[var] = sample_product(total, shift).astype(BF16)
     pl.semaphore_wait(barrier, len(everyone))
     pl.semaphore_signal(opposite_sem, 1, device_id=far_peers[1][1], device_id_type=MESH)
     for _, device in along_x:
         pl.semaphore_signal(diagonal_sem, 1, device_id=device, device_id_type=MESH)
     group = exchange_samples(0, p_first)
-    for b in range(NEAR):
-        g_t[b * PIECE : (b + 1) * PIECE, :] = g[:, b * PIECE : (b + 1) * PIECE].T
+    for i in range(LOADS):
+        g_t[i * step : (i + 1) * step, :] = g[:, i * step : (i + 1) * step].T
     wait(group)
-    arriving = variant_pass(0, total_of(p_first, N_VAR), part_1, near_1, far_1, whole_1)
-
-    group, whiten = sample_pass(0, whole_1, arriving)
+    arriving = variant_pass(0, total_of(p_first, N_VAR))
+
+    group, whiten = sample_pass(0, arriving)
     wait(group)
     sample_block = full(whiten, total_of(p_slots.at[0], N_VAR))
-    arriving = variant_pass(1, sample_block, part_2, near_2, far_2, whole_2)
-
-    group, whiten = sample_pass(1, whole_2, arriving)
+    arriving = variant_pass(1, sample_block)
+
+    group, whiten = sample_pass(1, arriving)
     scaled = whiten * jnp.sqrt(jnp.float32(VARIANTS))
-    for b in range(NEAR):
-        load_ref[:, b * PIECE : (b + 1) * PIECE] = full(scaled, whole_2[b].astype(F32))
+    for b in range(0, PARTS * NEAR, 4):
+        blocks = [whole[PARTS + b // NEAR, b % NEAR + i] for i in range(4)]
+        load_ref[:, b * PIECE : (b + 4) * PIECE] = full(scaled, jnp.concatenate(blocks, axis=1))
     wait(group)
     score_ref[...] = full(whiten, total_of(p_slots.at[1], N_VAR))
     for _, out, _ in sent:
@@ -263,7 +274,7 @@
 
 def local(genotypes, frequency, start_block):
     piece = (BLOCK, PIECE)
-    row = (NEAR, 1, PIECE)
+    row = (PARTS * NEAR, 1, PIECE)
     scratch = [
         pltpu.VMEM((ROWS, COLS), BF16),
         pltpu.VMEM((COLS, ROWS), BF16),
@@ -273,13 +284,13 @@
         pltpu.VMEM(row, F32),
         pltpu.VMEM((N_VAR, BLOCK, ROWS), BF16),
         pltpu.VMEM((2, N_VAR, BLOCK, ROWS), F32),
-        pltpu.VMEM((4, BLOCK, 128), F32),
+        pltpu.VMEM((4 * PARTS, BLOCK, 128), F32),
         pltpu.VMEM((2, N_VAR, BLOCK, 128), F32),
     ]
-    for wire in (FIRST_WIRE, SECOND_WIRE):
-        scratch += [pltpu.VMEM((n,) + piece, wire) for n in (NEAR, NEAR, FAR, NEAR)]
+    stages = 2 * PARTS
+    scratch += [pltpu.VMEM((stages, n) + piece, F32) for n in (NEAR, NEAR, FAR, NEAR)]
     scratch += [pltpu.SemaphoreType.DMA((LOADS + 2,))]
-    for n in ((3, N_VAR), (2, N_VAR), (2, NEAR), (2, FAR), (2, NEAR)):
+    for n in ((3, N_VAR), (2, N_VAR), (stages, NEAR), (stages, FAR), (stages, NEAR)):
         scratch += [pltpu.SemaphoreType.DMA(n)] * 2
     scratch += [pltpu.SemaphoreType.REGULAR] * 2
     vmem, hbm = pl.BlockSpec(memory_space=pltpu.VMEM), pl.BlockSpec(memory_space=pl.ANY)

time: 74.6 us -> 77.7 us (1.042)
  Pallas kernels: 72.5 us -> 75.5 us
    pallas_call x1, Pallas kernels: 72.5 us -> 75.5 us  [local(): pl.pallas_call(kernel, name='subspace', out_shape=(pltpu.VMEM((BLOCK, COL...]
where the time goes in v3:
time: 77.7 us; the launch traced here: 77.5 us
  Pallas kernels  75.5 us (97%)
  local copies, waits for them, and re-layouts  1.32 us (2%)
    pallas_call x1, Pallas kernels, local(): pl.pallas_call(kernel, name='subspace', out_shape=(pltpu.VMEM((BLOCK, COL...  75.5 us

profile of v3, /device:TPU:1, one launch (start us, length us, event | category | flops | bytes accessed | tf_op | source)
XLA Modules:
  0.0 77.5 jit_solution(14463224004029166273)
XLA Ops:
  0.6 75.5 %subspace.1 = (f32[16,4096]{1,0:T(8,128)S(1)}, f32[16,512]{1,0:T(8,128)S(1)}) custom-call(bf16[512,4096]{1,0:T(8,128)(2,1)} %g_hbm.1, f32[32,1,128]{2,1,0:T(1,128)} %bitcast.7, f32[16,4096]{1,0:T(8,128)} %bitcast.6), custom_call_target="tpu_custom_call" | custom-call | flops 335544320 | bytes 4194304 | tf_op jit(solution)/shard_map/subspace/pallas_call | solution.py:297
  76.2 0.7 copy.7
  76.9 0.6 copy.8

commit v4 on v3

v4 whole, which is shorter than its diff:
```python
import jax
import jax.numpy as jnp
from jax import lax
from jax.experimental import pallas as pl
from jax.experimental.pallas import tpu as pltpu
from jax.sharding import PartitionSpec as P

MESH = pl.DeviceIdType.MESH
F32, BF16 = jnp.float32, jnp.bfloat16
BLOCK = 16
VARIANTS = 32768
ROWS, COLS = 512, 4096
N_VAR = 8
NEAR, FAR = 16, 4
PARTS = (2, 1)
WIRE = (F32, BF16)
UNIT = 128
LOADS = 8


def split(a, terms):
    parts, rest = [], a
    for _ in range(terms):
        part = rest.astype(BF16)
        parts.append(part)
        rest = rest - part.astype(F32)
    return parts


def nt(a, b):
    return lax.dot_general(a, b, (((1,), (1,)), ((), ())), preferred_element_type=F32)


def full(a, b):
    return jnp.dot(a, b, precision=lax.Precision.HIGHEST, preferred_element_type=F32)


def row_of(a, k):
    return jnp.broadcast_to(a[k : k + 1, :], a.shape)


def spread(matrix):
    shape = (BLOCK, 128)
    columns = [jnp.broadcast_to(matrix[:, j : j + 1], shape) for j in range(BLOCK)]
    return columns, lax.broadcasted_iota(jnp.int32, shape, 0), lax.broadcasted_iota(jnp.int32, shape, 1)


def factorise(gram):
    columns, row, lane = spread(gram)
    inverse = jnp.where(row == lane, 1.0, 0.0).astype(F32)
    roots, lower = jnp.zeros_like(inverse), jnp.zeros_like(inverse)
    for k in range(BLOCK):
        column = columns[k]
        pivot = row_of(column, k)
        root = 1.0 / jnp.sqrt(pivot)
        factor = jnp.where(row > k, column / pivot, 0.0)
        roots = jnp.where(row == k, root, roots)
        lower = jnp.where((lane == k) & (row >= k), column * root, lower)
        for j in range(k + 1, BLOCK):
            columns[j] = columns[j] - factor * row_of(column, j)
        inverse = inverse - factor * row_of(inverse, k)
    return lower, inverse * roots


def decorrelated(expected, rows):
    columns, row, _ = spread(expected)
    for k in range(BLOCK - 1):
        column = columns[k]
        factor = jnp.where(row > k, column / row_of(column, k), 0.0)
        factor = jnp.where(jnp.abs(factor) <= 8.0, factor, 0.0)
        for j in range(k + 1, BLOCK):
            columns[j] = columns[j] - factor * row_of(column, j)
        rows = rows - factor * row_of(rows, k)
    return rows


def kernel(
    g_hbm, freq_hbm, start_hbm, load_ref, score_ref,
    g, g_t, start_block, frequency, centre, scale,
    p_narrow, p_wide, gram_rows, gram_slots, start_inverse,
    part_1, near_1, far_1, whole_1,
    part_2, near_2, far_2, whole_2,
    load_sems, pair_send, pair_recv, gram_send, gram_recv,
    near_send, near_recv, far_send, far_recv, whole_send, whole_recv, opposite_sem, diagonal_sem,
):
    samp, var = lax.axis_index("samp"), lax.axis_index("var")
    z, x = lax.div(samp, 4), lax.rem(samp, 4)
    z_far, z_near = lax.div(z, 4), lax.rem(z, 4)
    y, core = lax.div(var, 2), lax.rem(var, 2)
    my_near = z_near * 4 + x

    var_peers = []
    for dy in (2, 1, 3, 0):
        for dc in (0, 1):
            if dy or dc:
                other = lax.rem(y + dy, 4) * 2 + lax.rem(core + dc, 2)
                var_peers.append((other, (samp, other)))
    z_at = [z_near, z_near + 1 - 2 * lax.rem(z_near, 2), lax.rem(z_near + 2, 4), 3 - z_near]
    steps = [(a, b) for a in range(4) for b in range(4) if a or b]
    steps.sort(key=lambda step: -step[0] - (0, 1, 2, 1.6)[step[1]])
    near_peers = []
    for a, b in steps:
        slot = z_at[a] * 4 + lax.rem(x + b, 4)
        near_peers.append((slot, (z_far * 16 + slot, var)))
    far_peers = []
    for d in (2, 1, 3):
        slot = lax.rem(z_far + d, 4)
        far_peers.append((slot, (slot * 16 + my_near, var)))

    barrier = pltpu.get_barrier_semaphore()
    along_x = [near_peers[i] for i, (a, b) in enumerate(steps) if a == 0]
    along_z = [near_peers[i] for i, (a, b) in enumerate(steps) if b == 0]
    everyone = far_peers[1:] + along_z + along_x + var_peers
    for _, device in everyone:
        pl.semaphore_signal(barrier, 1, device_id=device, device_id_type=MESH)

    loads = [
        pltpu.make_async_copy(freq_hbm, frequency, load_sems.at[0]),
        pltpu.make_async_copy(start_hbm, start_block, load_sems.at[1]),
    ]
    step = COLS // LOADS
    for i in range(LOADS):
        columns = pl.ds(i * step, step)
        loads.append(pltpu.make_async_copy(g_hbm.at[:, columns], g.at[:, columns], load_sems.at[i + 2]))
    for load in loads:
        load.start()

    def copies(peers, source, target, mine, send, recv):
        return [
            (
                slot,
                pltpu.make_async_remote_copy(
                    src_ref=source(slot), dst_ref=target.at[mine], send_sem=send.at[slot], recv_sem=recv.at[mine],
                    device_id=device, device_id_type=MESH,
                ),
                pltpu.make_async_remote_copy(
                    src_ref=source(slot), dst_ref=target.at[slot], send_sem=send.at[slot], recv_sem=recv.at[slot],
                    device_id=device, device_id_type=MESH,
                ),
            )
            for slot, device in peers
        ]

    sent = []

    def start(group):
        for _, out, _ in group:
            out.start()
        sent.extend(group)

    def wait(group):
        for _, _, back in group:
            back.wait_recv()

    def units(ref, first, n):
        return jnp.concatenate([ref[first + i] for i in range(n)], axis=1)

    def scaled_terms(block, first):
        n = block.shape[1] // UNIT
        high, low = split(block * units(scale, first, n), 2)
        exact = (high.astype(F32) + low.astype(F32)) * units(centre, first, n)
        return jnp.concatenate([high, low], axis=0), jnp.sum(exact, axis=1, keepdims=True)

    def sample_product(total, shift):
        return total[0:BLOCK] + total[BLOCK:] - shift

    def exchange(slots, send, recv):
        group = copies(var_peers, lambda slot: slots.at[var], slots, var, send, recv)
        start(group)
        return group

    def exchange_gram(index, gram):
        slots = gram_slots.at[index]
        slots[var, :, 0:BLOCK] = gram
        slots[var, :, BLOCK:] = jnp.zeros((BLOCK, 128 - BLOCK), F32)
        return exchange(slots, gram_send.at[index], gram_recv.at[index])

    def gram_of(index, group):
        wait(group)
        return total_of(gram_slots.at[index], N_VAR)[:, 0:BLOCK]

    def total_of(slots, n):
        total = slots[0].astype(F32)
        for i in range(1, n):
            total = total + slots[i].astype(F32)
        return total

    blocks = ((part_1, near_1, far_1, whole_1), (part_2, near_2, far_2, whole_2))
    first_stage = (0, PARTS[0])

    def variant_pass(index, sample_block, meanwhile):
        part, near, far, whole = blocks[index]
        wire = part.dtype
        piece = part.shape[-1]
        chunk = max(piece, 2 * UNIT)
        narrow = sample_block.astype(BF16)
        shift = jnp.sum(narrow.astype(F32), axis=1, keepdims=True)
        groups = []
        for h in range(PARTS[index]):
            stage = first_stage[index] + h
            for b in range(0, NEAR * piece, chunk):
                first = h * NEAR * piece + b
                product = jnp.dot(narrow, g[:, first : first + chunk], preferred_element_type=F32)
                n = chunk // UNIT
                product = (product - shift * units(centre, first // UNIT, n)) * units(scale, first // UNIT, n)
                for i in range(chunk // piece):
                    part[h, b // piece + i] = product[:, i * piece : (i + 1) * piece].astype(wire)
            if stage == 0:
                pl.semaphore_wait(diagonal_sem, len(along_x))
            group = copies(
                near_peers, lambda slot: part.at[h, slot], near.at[h], my_near, near_send.at[stage], near_recv.at[stage]
            )
            start(group)
            groups.append(group)
        meanwhile()
        far_groups = []
        for h, group in enumerate(groups):
            stage = first_stage[index] + h
            total = part[h, my_near].astype(F32)
            for slot, _, back in reversed(group):
                back.wait_recv()
                total = total + near[h, slot].astype(F32)
            far[h, z_far] = total.astype(wire)
            if stage == 0:
                pl.semaphore_wait(opposite_sem, 1)
            group = copies(far_peers, lambda slot: far.at[h, z_far], far.at[h], z_far, far_send.at[stage], far_recv.at[stage])
            start(group)
            far_groups.append(group)
        groups = []
        for h, group in enumerate(far_groups):
            stage = first_stage[index] + h
            wait(group)
            whole[h, my_near] = total_of(far.at[h], FAR).astype(wire)
            group = copies(
                near_peers, lambda slot: whole.at[h, my_near], whole.at[h], my_near, whole_send.at[stage], whole_recv.at[stage]
            )
            start(group)
            groups.append(group)
        return groups

    def sample_pass(index, arriving, slots, send, recv):
        whole = blocks[index][-1]
        depth = 4 * whole.shape[-1]
        total, shift = jnp.zeros((2 * BLOCK, ROWS), F32), jnp.zeros((BLOCK, 1), F32)
        for h in range(PARTS[index]):
            for a in range(4):
                wait([arriving[h][i] for i, step in enumerate(steps) if step[0] == a])
                block = jnp.concatenate([whole[h, z_at[a] * 4 + i] for i in range(4)], axis=1)
                if whole.dtype == BF16:
                    left = right = block
                else:
                    high, middle, low = split(block, 3)
                    left = jnp.concatenate([high, high, middle, high, low, middle], axis=1)
                    right = jnp.concatenate([high, middle, high, low, high, middle], axis=1)
                place = h * 4 + z_at[a]
                gram_rows[place, :, 0:BLOCK] = nt(left, right)
                terms, shifted = scaled_terms(block.astype(F32), place * (depth // UNIT))
                shift = shift + shifted
                total = total + jnp.dot(
                    terms, g_t[pl.ds(pl.multiple_of(place * depth, depth), depth), :], preferred_element_type=F32
                )
        gram = gram_rows[0, :, 0:BLOCK]
        for i in range(1, 4 * PARTS[index]):
            gram = gram + gram_rows[i, :, 0:BLOCK]
        gram_group = exchange_gram(index + 1, gram)
        slots[var] = sample_product(total, shift).astype(slots.dtype)
        return exchange(slots, send, recv), factorise(gram_of(index + 1, gram_group))

    loads[0].wait()
    centre[...] = 2.0 * frequency[...]
    scale[...] = 1.0 / jnp.sqrt(centre[...] * (1.0 - frequency[...]))
    loads[1].wait()
    total, shift = jnp.zeros((2 * BLOCK, ROWS), F32), jnp.zeros((BLOCK, 1), F32)
    start_gram = jnp.zeros((BLOCK, BLOCK), F32)
    for i in range(LOADS):
        columns = slice(i * step, (i + 1) * step)
        narrow = start_block[:, columns].astype(BF16)
        start_gram = start_gram + nt(narrow, narrow)
        terms, shifted = scaled_terms(narrow.astype(F32), i * step // UNIT)
        shift = shift + shifted
        loads[i + 2].wait()
        total = total + nt(terms, g[:, columns])
    slots = p_narrow.at[0]
    slots[var] = sample_product(total, shift).astype(BF16)
    pl.semaphore_wait(barrier, len(everyone))
    pl.semaphore_signal(opposite_sem, 1, device_id=far_peers[1][1], device_id_type=MESH)
    for _, device in along_x:
        pl.semaphore_signal(diagonal_sem, 1, device_id=device, device_id_type=MESH)
    group = exchange(slots, pair_send.at[0], pair_recv.at[0])
    start_group = exchange_gram(0, start_gram)
    for i in range(LOADS):
        g_t[i * step : (i + 1) * step, :] = g[:, i * step : (i + 1) * step].T

    def factorise_start():
        start_inverse[...] = factorise(gram_of(0, start_group))[1]

    wait(group)
    arriving = variant_pass(0, total_of(slots, N_VAR), factorise_start)

    group, (lower, inverse) = sample_pass(0, arriving, p_wide, pair_send.at[1], pair_recv.at[1])
    relative = full(start_inverse[:, 0:BLOCK], lower[:, 0:BLOCK])
    expected = lax.dot_general(
        relative, relative, (((0,), (0,)), ((), ())), precision=lax.Precision.HIGHEST, preferred_element_type=F32
    )
    mixing = decorrelated(expected, inverse)[:, 0:BLOCK]
    wait(group)
    arriving = variant_pass(1, full(mixing, total_of(p_wide, N_VAR)), lambda: None)

    slots = p_narrow.at[1]
    group, (_, inverse) = sample_pass(1, arriving, slots, pair_send.at[2], pair_recv.at[2])
    inverse = inverse[:, 0:BLOCK]
    scaled = inverse * jnp.sqrt(jnp.float32(VARIANTS))
    piece = whole_2.shape[-1]
    for b in range(0, PARTS[1] * NEAR, 4):
        block = jnp.concatenate([whole_2[b // NEAR, b % NEAR + i].astype(F32) for i in range(4)], axis=1)
        load_ref[:, b * piece : (b + 4) * piece] = full(scaled, block)
    wait(group)
    score_ref[...] = full(inverse, total_of(slots, N_VAR))
    for _, out, _ in sent:
        out.wait_send()


def local(genotypes, frequency, start_block):
    row = (COLS // UNIT, 1, UNIT)
    scratch = [
        pltpu.VMEM((ROWS, COLS), BF16),
        pltpu.VMEM((COLS, ROWS), BF16),
        pltpu.VMEM((BLOCK, COLS), F32),
        pltpu.VMEM(row, F32),
        pltpu.VMEM(row, F32),
        pltpu.VMEM(row, F32),
        pltpu.VMEM((2, N_VAR, BLOCK, ROWS), BF16),
        pltpu.VMEM((N_VAR, BLOCK, ROWS), F32),
        pltpu.VMEM((4 * max(PARTS), BLOCK, 128), F32),
        pltpu.VMEM((3, N_VAR, BLOCK, 128), F32),
        pltpu.VMEM((BLOCK, 128), F32),
    ]
    for parts, wire in zip(PARTS, WIRE):
        scratch += [pltpu.VMEM((parts, n, BLOCK, COLS // NEAR // parts), wire) for n in (NEAR, NEAR, FAR, NEAR)]
    scratch += [pltpu.SemaphoreType.DMA((LOADS + 2,))]
    for n in ((3, N_VAR), (3, N_VAR), (sum(PARTS), NEAR), (sum(PARTS), FAR), (sum(PARTS), NEAR)):
        scratch += [pltpu.SemaphoreType.DMA(n)] * 2
    scratch += [pltpu.SemaphoreType.REGULAR] * 2
    vmem, hbm = pl.BlockSpec(memory_space=pltpu.VMEM), pl.BlockSpec(memory_space=pl.ANY)
    loadings, scores = pl.pallas_call(
        kernel,
        name="subspace",
        out_shape=(pltpu.VMEM((BLOCK, COLS), F32), pltpu.VMEM((BLOCK, ROWS), F32)),
        in_specs=[hbm, hbm, hbm],
        out_specs=(vmem, vmem),
        scratch_shapes=scratch,
        compiler_params=pltpu.CompilerParams(collective_id=0, has_side_effects=True, vmem_limit_bytes=48 << 20),
        cost_estimate=pl.CostEstimate(flops=5 * 2 * ROWS * COLS * BLOCK, bytes_accessed=2 * ROWS * COLS, transcendentals=0),
    )(*(pltpu.with_memory_space_constraint(a, pltpu.HBM) for a in (genotypes, frequency.reshape(row), start_block.T)))
    return loadings.T, scores.T


def solution(mesh):
    return jax.shard_map(
        local,
        mesh=mesh,
        in_specs=(P("samp", "var"), P("var"), P("var", None)),
        out_specs=(P("var", None), P("samp", None)),
        check_vma=False,
    )
```

time: 77.7 us -> 73.4 us (0.945)
  Pallas kernels: 75.5 us -> 71.3 us
    pallas_call x1, Pallas kernels: 75.5 us -> 71.3 us  [local(): pl.pallas_call(kernel, name='subspace', out_shape=(pltpu.VMEM((BLOCK, COL...]
where the time goes in v4:
time: 73.4 us; the launch traced here: 73.3 us
  Pallas kernels  71.3 us (97%)
  local copies, waits for them, and re-layouts  1.32 us (2%)
    pallas_call x1, Pallas kernels, local(): pl.pallas_call(kernel, name='subspace', out_shape=(pltpu.VMEM((BLOCK, COL...  71.3 us

profile of v4, /device:TPU:1, one launch (start us, length us, event | category | flops | bytes accessed | tf_op | source)
XLA Modules:
  0.0 73.3 jit_solution(11037821910253948227)
XLA Ops:
  0.6 71.3 %subspace.1 = (f32[16,4096]{1,0:T(8,128)S(1)}, f32[16,512]{1,0:T(8,128)S(1)}) custom-call(bf16[512,4096]{1,0:T(8,128)(2,1)} %g_hbm.1, f32[32,1,128]{2,1,0:T(1,128)} %bitcast.7, f32[16,4096]{1,0:T(8,128)} %bitcast.6), custom_call_target="tpu_custom_call" | custom-call | flops 335544320 | bytes 4194304 | tf_op jit(solution)/shard_map/subspace/pallas_call | solution.py:345
  71.9 0.7 copy.7
  72.7 0.6 copy.8

commit v5 on v4

--- a/solution.py
+++ b/solution.py
@@ -81,7 +81,7 @@
     part_1, near_1, far_1, whole_1,
     part_2, near_2, far_2, whole_2,
     load_sems, pair_send, pair_recv, gram_send, gram_recv,
-    near_send, near_recv, far_send, far_recv, whole_send, whole_recv, opposite_sem, diagonal_sem,
+    near_send, near_recv, far_send, far_recv, whole_send, whole_recv, far_sem, diagonal_sem,
 ):
     samp, var = lax.axis_index("samp"), lax.axis_index("var")
     z, x = lax.div(samp, 4), lax.rem(samp, 4)
@@ -110,9 +110,14 @@
     barrier = pltpu.get_barrier_semaphore()
     along_x = [near_peers[i] for i, (a, b) in enumerate(steps) if a == 0]
     along_z = [near_peers[i] for i, (a, b) in enumerate(steps) if b == 0]
-    everyone = far_peers[1:] + along_z + along_x + var_peers
+    everyone = along_z + along_x + var_peers
     for _, device in everyone:
         pl.semaphore_signal(barrier, 1, device_id=device, device_id_type=MESH)
+
+    @pl.when(z_far != 2)
+    def _():
+        pl.semaphore_signal(barrier, 1, device_id=(2 * NEAR + my_near, var), device_id_type=MESH)
+
 
     loads = [
         pltpu.make_async_copy(freq_hbm, frequency, load_sems.at[0]),
@@ -171,13 +176,16 @@
 
     def exchange_gram(index, gram):
         slots = gram_slots.at[index]
-        slots[var, :, 0:BLOCK] = gram
-        slots[var, :, BLOCK:] = jnp.zeros((BLOCK, 128 - BLOCK), F32)
+        half = BLOCK // 2
+        slots[var, :, 0:BLOCK] = gram[0:half]
+        slots[var, :, BLOCK : 2 * BLOCK] = gram[half:]
+        slots[var, :, 2 * BLOCK :] = jnp.zeros((half, 128 - 2 * BLOCK), F32)
         return exchange(slots, gram_send.at[index], gram_recv.at[index])
 
     def gram_of(index, group):
         wait(group)
-        return total_of(gram_slots.at[index], N_VAR)[:, 0:BLOCK]
+        total = total_of(gram_slots.at[index], N_VAR)
+        return jnp.concatenate([total[:, 0:BLOCK], total[:, BLOCK : 2 * BLOCK]], axis=0)
 
     def total_of(slots, n):
         total = slots[0].astype(F32)
@@ -222,7 +230,11 @@
                 total = total + near[h, slot].astype(F32)
             far[h, z_far] = total.astype(wire)
             if stage == 0:
-                pl.semaphore_wait(opposite_sem, 1)
+
+                @pl.when(z_far != 2)
+                def _():
+                    pl.semaphore_wait(far_sem, 1)
+
             group = copies(far_peers, lambda slot: far.at[h, z_far], far.at[h], z_far, far_send.at[stage], far_recv.at[stage])
             start(group)
             far_groups.append(group)
@@ -282,8 +294,17 @@
         total = total + nt(terms, g[:, columns])
     slots = p_narrow.at[0]
     slots[var] = sample_product(total, shift).astype(BF16)
-    pl.semaphore_wait(barrier, len(everyone))
-    pl.semaphore_signal(opposite_sem, 1, device_id=far_peers[1][1], device_id_type=MESH)
+
+    @pl.when(z_far != 2)
+    def _():
+        pl.semaphore_wait(barrier, len(everyone))
+
+    @pl.when(z_far == 2)
+    def _():
+        pl.semaphore_wait(barrier, len(everyone) + len(far_peers))
+        for _, device in far_peers:
+            pl.semaphore_signal(far_sem, 1, device_id=device, device_id_type=MESH)
+
     for _, device in along_x:
         pl.semaphore_signal(diagonal_sem, 1, device_id=device, device_id_type=MESH)
     group = exchange(slots, pair_send.at[0], pair_recv.at[0])
@@ -309,14 +330,17 @@
     slots = p_narrow.at[1]
     group, (_, inverse) = sample_pass(1, arriving, slots, pair_send.at[2], pair_recv.at[2])
     inverse = inverse[:, 0:BLOCK]
-    scaled = inverse * jnp.sqrt(jnp.float32(VARIANTS))
+    scaled = jnp.concatenate(split(inverse * jnp.sqrt(jnp.float32(VARIANTS)), 3), axis=0)
     piece = whole_2.shape[-1]
     for b in range(0, PARTS[1] * NEAR, 4):
-        block = jnp.concatenate([whole_2[b // NEAR, b % NEAR + i].astype(F32) for i in range(4)], axis=1)
-        load_ref[:, b * piece : (b + 4) * piece] = full(scaled, block)
+        block = jnp.concatenate([whole_2[b // NEAR, b % NEAR + i] for i in range(4)], axis=1)
+        terms = jnp.dot(scaled, block, preferred_element_type=F32)
+        load_ref[:, b * piece : (b + 4) * piece] = (terms[2 * BLOCK :] + terms[BLOCK : 2 * BLOCK]) + terms[0:BLOCK]
+    for _, out, _ in sent[: -len(group)]:
+        out.wait_send()
     wait(group)
     score_ref[...] = full(inverse, total_of(slots, N_VAR))
-    for _, out, _ in sent:
+    for _, out, _ in group:
         out.wait_send()
 
 
@@ -332,7 +356,7 @@
         pltpu.VMEM((2, N_VAR, BLOCK, ROWS), BF16),
         pltpu.VMEM((N_VAR, BLOCK, ROWS), F32),
         pltpu.VMEM((4 * max(PARTS), BLOCK, 128), F32),
-        pltpu.VMEM((3, N_VAR, BLOCK, 128), F32),
+        pltpu.VMEM((3, N_VAR, BLOCK // 2, 128), F32),
         pltpu.VMEM((BLOCK, 128), F32),
     ]
     for parts, wire in zip(PARTS, WIRE):

time: 73.4 us -> 72.5 us (0.988)
  Pallas kernels: 71.3 us -> 70.3 us
    pallas_call x1, Pallas kernels: 71.3 us -> 70.3 us  [local(): pl.pallas_call(kernel, name='subspace', out_shape=(pltpu.VMEM((BLOCK, COL...]
where the time goes in v5:
time: 72.5 us; the launch traced here: 72.3 us
  Pallas kernels  70.3 us (97%)
  local copies, waits for them, and re-layouts  1.32 us (2%)
    pallas_call x1, Pallas kernels, local(): pl.pallas_call(kernel, name='subspace', out_shape=(pltpu.VMEM((BLOCK, COL...  70.3 us

profile of v5, /device:TPU:1, one launch (start us, length us, event | category | flops | bytes accessed | tf_op | source)
XLA Modules:
  0.0 72.3 jit_solution(4919953888261290012)
XLA Ops:
  0.6 70.3 %subspace.1 = (f32[16,4096]{1,0:T(8,128)S(1)}, f32[16,512]{1,0:T(8,128)S(1)}) custom-call(bf16[512,4096]{1,0:T(8,128)(2,1)} %g_hbm.1, f32[32,1,128]{2,1,0:T(1,128)} %bitcast.7, f32[16,4096]{1,0:T(8,128)} %bitcast.6), custom_call_target="tpu_custom_call" | custom-call | flops 335544320 | bytes 4194304 | tf_op jit(solution)/shard_map/subspace/pallas_call | solution.py:369
  71.0 0.7 copy.7
  71.7 0.6 copy.8
